TPU v7x, 32 devices: a whole 2x2x4 slice. The times are simulated.
32 devices in a mesh: dp: 4 (over y, core), tensor: 8 (over z, x).
Axes of the slice: x: 2, y: 2, z: 4, core: 2. Of those that a mesh axis runs over, the one named last changes fastest.
Arguments:
- hidden: bfloat16 [1024, 14336], P('dp', 'tensor'), may hold values from -6 to 6
- residual: bfloat16 [1024, 8192], P('tensor', 'dp'), may hold values from -6 to 6
- master: float32 [14336, 8192], P('tensor', 'dp'), may hold values from -0.046875 to 0.046875
- moment: float32 [14336, 8192], P('tensor', 'dp'), may hold values from -0.00021362305 to 0.00021362305
- second: float32 [14336, 8192], P('tensor', 'dp'), as said below
- gain: float32 [8192], P('dp'), may hold values from 0.5 to 1.5
- head: float32 [8192], P('dp')
- lengths: int32 [4, 2], replicated, may hold values from 32 to 128, as said below
- labels: int32 [4], replicated, may hold values from 0 to 1
Outputs:
- new_master: float32 [14336, 8192], P('tensor', 'dp')
- new_moment: float32 [14336, 8192], P('tensor', 'dp')
- new_second: float32 [14336, 8192], P('tensor', 'dp')
- loss: float32 [], replicated
Inputs may be any that keep to these rules, and one draw needn't show every extreme that they name: `lengths`: some sequence has exactly 128 valid tokens in every draw; every sequence has at least 32. `second`: Positive.
All inputs are finite; a program needn't handle non-finite values.
Results may differ from a plain program's by a relative error of at most 0.015.
Values may be sent and summed in bfloat16 or wider, within the bound.
A program may use at most 192 MiB of HBM per device.

v0:
```python
import jax
import jax.numpy as jnp
from jax import lax
from jax.sharding import PartitionSpec as P

D = 8192
LEN = 128
STEP = 100


EPS_NORM = 1e-05


def width_sums(stream, w_vec):
    squares = jnp.sum(stream * stream, 1)
    product = jnp.sum(stream * w_vec[None, :], 1)
    return lax.psum((squares, product), "dp")


def per_device(hidden, residual, master, moment, second, gain, head, lengths, labels):
    t_index = lax.axis_index("tensor")
    block_rows = residual.shape[0]
    weights = master.astype(jnp.bfloat16)
    gathered = lax.all_gather(hidden, "dp", axis=0, tiled=True)
    partial_value = jnp.dot(gathered, weights, preferred_element_type=jnp.float32)
    row_start = t_index * block_rows
    own = lax.dynamic_slice_in_dim(partial_value, row_start, block_rows, 0) + residual.astype(
        jnp.float32
    )
    term = lax.dynamic_update_slice_in_dim(partial_value, own, row_start, 0)
    w_vec = gain * head
    lens_flat = lengths.reshape(-1)
    seq_count = lens_flat.shape[0]
    stream = lax.psum_scatter(
        term.astype(jnp.bfloat16), "tensor", scatter_dimension=0, tiled=True
    ).astype(jnp.float32)
    squares, product = width_sums(stream, w_vec)
    rows_here = stream.shape[0]
    row_ids = row_start + jnp.arange(rows_here, dtype=jnp.int32)
    seq_ids = row_ids // LEN
    position = row_ids % LEN
    member = seq_ids[:, None] == jnp.arange(seq_count, dtype=jnp.int32)[None, :]
    len_row = jnp.sum(jnp.where(member, lens_flat[None, :], 0), 1)
    valid = position < len_row
    rstd = lax.rsqrt(squares / D + EPS_NORM)
    score = rstd * product
    seq_part = jnp.sum(jnp.where(member & valid[:, None], score[:, None], 0.0), 0)
    seq_total = lax.psum(seq_part, "tensor")
    reward = (seq_total / lens_flat.astype(jnp.float32)).reshape(-1, 2)
    chosen = jnp.where(labels == 1, reward[:, 1], reward[:, 0])
    other = jnp.where(labels == 1, reward[:, 0], reward[:, 1])
    margin = chosen - other
    loss = jnp.sum(jax.nn.softplus(-margin))
    sig = jax.nn.sigmoid(-margin)
    first = jnp.where(labels == 0, -sig, sig)
    dreward = jnp.stack([first, -first], 1).reshape(-1)
    grad_row = jnp.sum(jnp.where(member, dreward[None, :], 0.0), 1)
    coef = jnp.where(valid, grad_row / len_row.astype(jnp.float32), 0.0)
    cotangent = (
        coef[:, None] * (rstd[:, None] * w_vec[None, :] - (product * rstd**3 / D)[:, None] * stream)
    ).astype(jnp.bfloat16)
    cotangent_all = lax.all_gather(cotangent, "tensor", axis=0, tiled=True)
    contract = (((0,), (0,)), ((), ()))
    grad = lax.dot_general(gathered, cotangent_all, contract, preferred_element_type=jnp.float32)
    new_moment = 0.9 * moment + 0.1 * grad
    new_second = 0.95 * second + 0.05 * grad * grad
    m_hat = new_moment / (1.0 - 0.9**STEP)
    v_hat = new_second / (1.0 - 0.95**STEP)
    new_master = master - 0.001 * (m_hat / (jnp.sqrt(v_hat) + 1e-08) + 0.1 * master)
    return (new_master, new_moment, new_second, loss)


def solution(mesh):
    return jax.shard_map(
        per_device,
        mesh=mesh,
        in_specs=(
            P("dp", "tensor"),
            P("tensor", "dp"),
            P("tensor", "dp"),
            P("tensor", "dp"),
            P("tensor", "dp"),
            P("dp"),
            P("dp"),
            P(),
            P(),
        ),
        out_specs=(P("tensor", "dp"), P("tensor", "dp"), P("tensor", "dp"), P()),
        check_vma=False,
    )
```

profile of v0, /device:TPU:0, one launch (start us, length us, event | category | flops | bytes accessed | tf_op | source)
XLA Modules:
  0.0 338.0 jit_solution(18259654686614337475)
XLA Ops:
  7.2 0.7 all-gather.3.cloned.1.call-update
  8.0 35.8 %all-gather.3.cloned.1.call-done = bf16[1024,1792]{1,0:T(8,128)(2,1)} async-done(((bf16[256,1792]{1,0:T(8,128)(2,1)}), bf16[1024,1792]{1,0:T(8,128)(2,1)}) %all-gather.3.cloned.1.call-update) | async-done | bytes 3670032 | tf_op jit(solution)/shard_map/all_gather | solution.py:24
  43.8 12.1 %fusion.2 = f32[1024,2048]{1,0:T(8,128)S(1)} fusion(bf16[1024,1792]{1,0:T(8,128)(2,1)} %all-gather.3.cloned.1.call-done, f32[1792,2048]{1,0:T(8,128)} %param.11), kind=kOutput, calls=%fused_computation.5 | convolution fusion | flops 7519862784 | bytes 26738688 | tf_op jit(solution)/shard_map/dot_general | solution.py:25
  55.9 0.2 add_dynamic-update-slice_fusion
  56.1 2.7 convert_element_type.27
  58.9 0.1 copy.32
  59.2 87.7 %reduce-scatter.2.cloned.1.call-done = bf16[128,2048]{1,0:T(8,128)(2,1)} async-done(((bf16[1024,2048]{1,0:T(8,128)(2,1)}), bf16[128,2048]{1,0:T(8,128)(2,1)}) %reduce-scatter.2.cloned.1.call-update) | async-done | bytes 524304 | tf_op jit(solution)/shard_map/reduce_scatter | solution.py:34
  146.9 1.3 fusion.4
  148.2 6.8 %all-reduce = (f32[128]{0:T(128)S(1)}, f32[128]{0:T(128)S(1)}) all-reduce(f32[128]{0:T(128)S(1)} %get-tuple-element.17, f32[128]{0:T(128)S(1)} %get-tuple-element.16), channel_id=1, replica_groups=mesh['dp'=4,'tensor'=8] {'dp'}, use_global_device_ids=true, to_apply=%region_5.6 | all-reduce | flops 256 | bytes 2048 | tf_op jit(solution)/shard_map/psum | solution.py:17
  155.0 0.1 select_reduce_fusion.1
  155.1 20.2 %psum.23 = f32[8]{0:T(128)S(1)} all-reduce(f32[8]{0:T(128)S(1)} %select_reduce_fusion.1), channel_id=1, replica_groups=mesh['dp'=4,'tensor'=8] {'tensor'}, use_global_device_ids=true, to_apply=%region_7.8 | all-reduce | flops 8 | bytes 64 | tf_op jit(solution)/shard_map/psum | solution.py:48
  175.4 0.2 slice_reduce_fusion
  175.6 0.6 fusion.13
  176.3 0.1 copy.33
  176.5 0.1 select_reduce_fusion
  176.6 2.1 fusion.8
  178.7 14.3 %copy.36 = f32[1792,2048]{0,1:T(8,128)} copy(f32[1792,2048]{1,0:T(8,128)} %param.11) | data formatting | bytes 29360128 | tf_op args[2]
  193.0 14.3 %copy.31 = f32[1792,2048]{0,1:T(8,128)} copy(f32[1792,2048]{1,0:T(8,128)} %param.12) | data formatting | bytes 29360128 | tf_op args[3]
  207.3 14.3 %copy.34 = f32[1792,2048]{0,1:T(8,128)} copy(f32[1792,2048]{1,0:T(8,128)} %param.13) | data formatting | bytes 29360128 | tf_op args[4]
  221.7 26.9 %all-gather.5.cloned.1.call-done = bf16[1024,2048]{1,0:T(8,128)(2,1)} async-done(((bf16[128,2048]{1,0:T(8,128)(2,1)}), bf16[1024,2048]{1,0:T(8,128)(2,1)}) %all-gather.5.cloned.1.call-update) | async-done | bytes 4194320 | tf_op jit(solution)/shard_map/all_gather | solution.py:62
  248.6 37.3 %multiply_subtract_fusion = (f32[1792,2048]{0,1:T(8,128)}, f32[1792,2048]{0,1:T(8,128)}, f32[1792,2048]{0,1:T(8,128)}) fusion(f32[1792,2048]{0,1:T(8,128)} %copy.36, f32[1792,2048]{0,1:T(8,128)} %copy.31, f32[1792,2048]{0,1:T(8,128)} %copy.34, bf16[1024,2048]{1,0:T(8,128)(2,1)} %all-gather.5.cloned.1.call-done, ...), kind=kOutput, calls=%fused_computation.4 | convolution fusion | flops 7571243008 | bytes 95944704 | tf_op jit(solution)/shard_map/dot_general | solution.py:64
  285.9 15.2 %copy.37 = f32[1792,2048]{1,0:T(8,128)} copy(f32[1792,2048]{0,1:T(8,128)} %get-tuple-element.24) | data formatting | bytes 29360128
  301.1 15.2 %copy.38 = f32[1792,2048]{1,0:T(8,128)} copy(f32[1792,2048]{0,1:T(8,128)} %get-tuple-element.25) | data formatting | bytes 29360128
  316.3 15.2 %copy.39 = f32[1792,2048]{1,0:T(8,128)} copy(f32[1792,2048]{0,1:T(8,128)} %get-tuple-element.26) | data formatting | bytes 29360128
  (27 shorter events, 0.6 us)
Async XLA Ops:
  7.2 36.6 %all-gather.3.cloned.1.call-start = ((), (), s32[]{:S(2)}) async-start(), calls=%async_computation.1 | async-start | bytes 4587520 | tf_op jit(solution)/shard_map/all_gather | solution.py:24
  7.9 139.0 %reduce-scatter.2.cloned.1.call-start = ((), (), s32[]{:S(2)}) async-start(), calls=%async_computation.2 | async-start | bytes 4718592 | tf_op jit(solution)/shard_map/reduce_scatter | solution.py:34
  8.0 47.9 %copy-start = (bf16[128,2048]{1,0:T(8,128)(2,1)S(1)}, bf16[128,2048]{1,0:T(8,128)(2,1)}, u32[]{:S(2)}) copy-start(bf16[128,2048]{1,0:T(8,128)(2,1)} %param.10) | copy-start | bytes 1572868
  55.9 3.0 copy-start.4
  55.9 3.2 copy-start.1
  55.9 3.2 copy-start.2
  55.9 119.7 %copy-start.3 = (s32[4]{0:T(128)S(1)}, s32[4]{0:T(128)}, u32[]{:S(2)}) copy-start(s32[4]{0:T(128)} %param.17) | copy-start | bytes 52
  58.8 189.8 %all-gather.5.cloned.1.call-start = ((), (), s32[]{:S(2)}) async-start(), calls=%async_computation.3 | async-start | bytes 4718592 | tf_op jit(solution)/shard_map/all_gather | solution.py:62
Sparse Core Ops, SparseCore 0:
  9.6 34.1 all-gather.2
  58.9 87.8 reduce-scatter.1
  178.8 69.6 all-gather.4
where the time goes:
time: 339 us; the launch traced here: 338 us
  waiting for transfers between devices  151 us (45%)
  local copies, waits for them, and re-layouts  89.1 us (26%)
  matrix products  49.4 us (15%)
  blocking collectives  27 us (8%)
  between operations  13.9 us (4%)
  other arithmetic  7.28 us (2%)
    unnamed x17, local copies, waits for them, and re-layouts  88.6 us
    reduce_scatter x1, waiting for transfers between devices, per_device(): lax.psum_scatter(term.astype(jnp.bfloat16), 'tensor', scatter_dimension=0...  87.7 us
    dot_general x1, matrix products, per_device(): lax.dot_general(gathered, cotangent_all, contract, preferred_element_type...  37.3 us
    all_gather x1, waiting for transfers between devices, per_device(): gathered = lax.all_gather(hidden, 'dp', axis=0, tiled=True)  35.8 us
    all_gather x1, waiting for transfers between devices, per_device(): cotangent_all = lax.all_gather(cotangent, 'tensor', axis=0, tiled=True)  26.9 us
    psum x1, blocking collectives, per_device(): seq_total = lax.psum(seq_part, 'tensor')  20.2 us
    dot_general x1, matrix products, per_device(): jnp.dot(gathered, weights, preferred_element_type=jnp.float32)  12.1 us
    psum x1, blocking collectives, width_sums(): return lax.psum((squares, product), 'dp')  6.84 us
  transfers between devices with their start and end apart: 3, of which 3 were waited for; matrix products, arithmetic and copies ran while one was open for 13% of the time, Pallas kernels for 0%

commit v1 on v0

v1 whole, which is shorter than its diff:
```python
import functools

import jax
import jax.numpy as jnp
from jax import lax
from jax.experimental import pallas as pl
from jax.experimental.pallas import tpu as pltpu
from jax.sharding import PartitionSpec as P

LEN = 128
STEP = 100
EPS_NORM = 1e-05
MIB = 1024 * 1024


def update_kernel(h_ref, s_ref, a_ref, b_ref, w_ref, p_ref, m_ref, v_ref, po_ref, mo_ref, vo_ref, cot):
    @pl.when(pl.program_id(0) == 0)
    def _():
        def fill(i, carry):
            rows = pl.ds(pl.multiple_of(i * 64, 64), 64)
            value = a_ref[rows, :] * w_ref[...] - b_ref[rows, :] * s_ref[rows, :].astype(jnp.float32)
            cot[rows, :] = value.astype(jnp.bfloat16)
            return carry

        lax.fori_loop(0, cot.shape[0] // 64, fill, 0)

    h = h_ref[...]
    wide = cot.shape[1]
    step = 512
    for c in range(wide // step):
        cols = slice(c * step, (c + 1) * step)
        grad = lax.dot_general(
            h, cot[:, cols], (((0,), (0,)), ((), ())), preferred_element_type=jnp.float32
        )
        moment = 0.9 * m_ref[:, cols] + 0.1 * grad
        second = 0.95 * v_ref[:, cols] + 0.05 * grad * grad
        mo_ref[:, cols] = moment
        vo_ref[:, cols] = second
        m_hat = moment * (1.0 / (1.0 - 0.9**STEP))
        v_hat = second * (1.0 / (1.0 - 0.95**STEP))
        master = p_ref[:, cols]
        po_ref[:, cols] = master - 0.001 * (m_hat / (jnp.sqrt(v_hat) + 1e-08) + 0.1 * master)


def update(hidden, stream, a, b, w, master, moment, second):
    tokens, ff = hidden.shape
    wide = stream.shape[1]
    tile = 128
    state = pl.BlockSpec((tile, wide), lambda i: (i, 0))
    whole = lambda x: pl.BlockSpec(x.shape, lambda i: (0, 0), pipeline_mode=pl.Buffered(1))
    out = jax.ShapeDtypeStruct(master.shape, jnp.float32)
    return pl.pallas_call(
        update_kernel,
        grid=(ff // tile,),
        in_specs=[pl.BlockSpec((tokens, tile), lambda i: (0, i))]
        + [whole(x) for x in (stream, a, b, w)]
        + [state] * 3,
        out_specs=[state] * 3,
        out_shape=[out] * 3,
        scratch_shapes=[pltpu.VMEM(stream.shape, jnp.bfloat16)],
        compiler_params=pltpu.CompilerParams(vmem_limit_bytes=48 * MIB),
        cost_estimate=pl.CostEstimate(
            flops=2 * tokens * ff * wide, bytes_accessed=24 * ff * wide, transcendentals=ff * wide
        ),
    )(hidden, stream, a, b, w, master, moment, second)


def row_terms(stream, w, lengths, labels, full_width):
    value = stream.astype(jnp.float32)
    sums = jnp.stack([jnp.sum(value * value, 1), jnp.sum(value * w[None, :], 1)])
    squares, product = lax.psum(sums, "dp")
    lens = lengths.reshape(-1)
    lens_f = lens.astype(jnp.float32)[:, None]
    valid = jnp.arange(LEN, dtype=jnp.int32)[None, :] < lens[:, None]
    squares = squares.reshape(-1, LEN)
    product = product.reshape(-1, LEN)
    rstd = lax.rsqrt(squares / full_width + EPS_NORM)
    total = jnp.sum(jnp.where(valid, rstd * product, 0.0), 1)
    reward = (total / lens_f[:, 0]).reshape(-1, 2)
    chosen = jnp.where(labels == 1, reward[:, 1], reward[:, 0])
    other = jnp.where(labels == 1, reward[:, 0], reward[:, 1])
    margin = chosen - other
    loss = jnp.sum(jax.nn.softplus(-margin))
    sig = jax.nn.sigmoid(-margin)
    first = jnp.where(labels == 0, -sig, sig)
    dreward = jnp.stack([first, -first], 1).reshape(-1, 1)
    coef = jnp.where(valid, dreward / lens_f, 0.0)
    a = (coef * rstd).reshape(-1, 1)
    b = (coef * (product * rstd**3 / full_width)).reshape(-1, 1)
    return a, b, loss


def per_device(dp, tensor, hidden, residual, master, moment, second, gain, head, lengths, labels):
    t_index = lax.axis_index("tensor")
    block_rows = residual.shape[0]
    gathered = lax.all_gather(hidden, "dp", axis=0, tiled=True)
    partial_value = jnp.dot(gathered, master.astype(jnp.bfloat16), preferred_element_type=jnp.float32)
    row_start = t_index * block_rows
    own = lax.dynamic_slice_in_dim(partial_value, row_start, block_rows, 0) + residual.astype(
        jnp.float32
    )
    term = lax.dynamic_update_slice_in_dim(partial_value, own, row_start, 0).astype(jnp.bfloat16)
    part = lax.psum_scatter(term, "tensor", scatter_dimension=0, tiled=True)
    stream = lax.all_gather(part, "tensor", axis=0, tiled=True)
    w = gain * head
    a, b, loss = row_terms(stream, w, lengths, labels, w.shape[0] * dp)
    new_master, new_moment, new_second = update(
        gathered, stream, a, b, w[None, :], master, moment, second
    )
    return new_master, new_moment, new_second, loss


def solution(mesh):
    state = P("tensor", "dp")
    return jax.shard_map(
        functools.partial(per_device, mesh.shape["dp"], mesh.shape["tensor"]),
        mesh=mesh,
        in_specs=(P("dp", "tensor"), state, state, state, state, P("dp"), P("dp"), P(), P()),
        out_specs=(state, state, state, P()),
        check_vma=False,
    )
```

time: 339 us -> 286 us (0.84)
  local copies, waits for them, and re-layouts: 89.1 us -> 3.82 us
  waiting for transfers between devices: 151 us -> 200 us
  Pallas kernels: 0 us -> 43.1 us
  matrix products: 49.4 us -> 12.1 us
  blocking collectives: 27 us -> 5.77 us
    unnamed x17 -> x13, local copies, waits for them, and re-layouts: 88.6 us -> 2.15 us
    all_gather x1, waiting for transfers between devices: 26.9 us -> 75.3 us  [per_device(): stream = lax.all_gather(part, 'tensor', axis=0, tiled=True)]
    pallas_call x0 -> x1, Pallas kernels: none -> 43.1 us  [update(): pl.pallas_call(update_kernel, grid=(ff // tile,), in_specs=[pl.BlockSpec(...]
    dot_general x2 -> x1, matrix products: 49.4 us -> 12.1 us  [per_device(): jnp.dot(gathered, master.astype(jnp.bfloat16), preferred_element_type=jnp...]
    psum x2 -> x1, blocking collectives: 27 us -> 5.77 us  [row_terms(): squares, product = lax.psum(sums, 'dp')]
  transfers between devices with their start and end apart: 3 -> 3, of which waited for: 3 -> 3; matrix products, arithmetic and copies ran while one was open for 13% -> 0% of each run, Pallas kernels for 0% -> 0%
where the time goes in v1:
time: 286 us
  waiting for transfers between devices  200 us (70%)
  Pallas kernels  43.1 us (15%)
  between operations  13.9 us (5%)
  matrix products  12.1 us (4%)
  other arithmetic  7.58 us (3%)
  blocking collectives  5.77 us (2%)
  local copies, waits for them, and re-layouts  3.82 us (1%)
    reduce_scatter x1, waiting for transfers between devices, per_device(): part = lax.psum_scatter(term, 'tensor', scatter_dimension=0, tiled=True)  88 us
    all_gather x1, waiting for transfers between devices, per_device(): stream = lax.all_gather(part, 'tensor', axis=0, tiled=True)  75.3 us
    pallas_call x1, Pallas kernels, update(): pl.pallas_call(update_kernel, grid=(ff // tile,), in_specs=[pl.BlockSpec(...  43.1 us
    all_gather x1, waiting for transfers between devices, per_device(): gathered = lax.all_gather(hidden, 'dp', axis=0, tiled=True)  35.8 us
    dot_general x1, matrix products, per_device(): jnp.dot(gathered, master.astype(jnp.bfloat16), preferred_element_type=jnp...  12.1 us
    psum x1, blocking collectives, row_terms(): squares, product = lax.psum(sums, 'dp')  5.77 us
  transfers between devices with their start and end apart: 3, of which 3 were waited for; matrix products, arithmetic and copies ran while one was open for 0% of the time, Pallas kernels for 0%

profile of v1, /device:TPU:0, one launch (start us, length us, event | category | flops | bytes accessed | tf_op | source)
XLA Modules:
  0.0 286.2 jit_solution(16910762240029693248)
XLA Ops:
  7.2 0.7 all-gather.3.cloned.1.call-update
  8.0 35.8 %all-gather.3.cloned.1.call-done.h_ref = bf16[1024,1792]{1,0:T(8,128)(2,1)} async-done(((bf16[256,1792]{1,0:T(8,128)(2,1)}), bf16[1024,1792]{1,0:T(8,128)(2,1)}) %all-gather.3.cloned.1.call-update) | async-done | bytes 3670032 | tf_op jit(solution)/shard_map/all_gather | solution.py:96
  43.8 12.1 %fusion.2 = f32[1024,2048]{1,0:T(8,128)S(1)} fusion(bf16[1024,1792]{1,0:T(8,128)(2,1)} %all-gather.3.cloned.1.call-done.h_ref, f32[1792,2048]{1,0:T(8,128)} %p_ref.1), kind=kOutput, calls=%fused_computation.4 | convolution fusion | flops 7519862784 | bytes 26738688 | tf_op jit(solution)/shard_map/dot_general | solution.py:97
  55.9 0.2 add_dynamic-update-slice_fusion
  56.1 2.7 convert_element_type.24
  58.9 88.0 %reduce-scatter.2.cloned.1.call-done = bf16[128,2048]{1,0:T(8,128)(2,1)} async-done(((bf16[1024,2048]{1,0:T(8,128)(2,1)}), bf16[128,2048]{1,0:T(8,128)(2,1)}) %reduce-scatter.2.cloned.1.call-update) | async-done | bytes 524304 | tf_op jit(solution)/shard_map/reduce_scatter | solution.py:103
  146.9 0.1 copy.26
  147.0 0.1 lt.37
  147.1 75.3 %all-gather.5.cloned.1.call-done.s_ref = bf16[1024,2048]{1,0:T(8,128)(2,1)} async-done(((bf16[128,2048]{1,0:T(8,128)(2,1)}), bf16[1024,2048]{1,0:T(8,128)(2,1)}) %all-gather.5.cloned.1.call-update) | async-done | bytes 4194320 | tf_op jit(solution)/shard_map/all_gather | solution.py:104
  222.4 3.7 %fusion = (f32[1024]{0:T(1024)S(1)}, f32[1024]{0:T(1024)S(1)}) fusion(bf16[1024,2048]{1,0:T(8,128)(2,1)} %all-gather.5.cloned.1.call-done.s_ref, f32[2048]{0:T(1024)S(1)} %mul.59), kind=kLoop, calls=%fused_computation.2 | loop fusion | flops 10483712 | bytes 4210688 | tf_op jit(solution)/shard_map/reduce_sum | solution.py:70
  226.1 5.8 %psum.7 = f32[2,1024]{1,0:T(2,128)S(1)} all-reduce(f32[2,1024]{1,0:T(2,128)S(1)} %pad_maximum_fusion), channel_id=1, replica_groups=mesh['dp'=4,'tensor'=8] {'dp'}, use_global_device_ids=true, to_apply=%region_3.0 | all-reduce | flops 2048 | bytes 16384 | tf_op jit(solution)/shard_map/psum | solution.py:71
  231.9 0.2 select_reduce_fusion
  232.2 0.2 slice_reduce_fusion
  232.4 0.6 fusion.8
  233.0 0.1 copy.28
  233.1 0.1 reshape.148
  233.3 0.2 copy.32
  233.5 0.2 copy.33.a_ref
  233.8 0.2 copy.31
  234.0 0.2 copy.29
  234.2 0.2 copy.30
  234.5 0.1 multiply_multiply_fusion.b_ref
  234.6 2.0 copy-done
  236.6 43.1 %shard_map.120 = (f32[1792,2048]{1,0:T(8,128)}, f32[1792,2048]{1,0:T(8,128)}, f32[1792,2048]{1,0:T(8,128)}) custom-call(bf16[1024,1792]{1,0:T(8,128)(2,1)S(1)} %copy-done, bf16[1024,2048]{1,0:T(8,128)(2,1)} %all-gather.5.cloned.1.call-done.s_ref, f32[1024,1]{1,0:T(8,128)S(1)} %copy.33.a_ref, f32[1024,1]{1,0:T(8,128)S(1)} %multiply_multiply_fusion.b_ref, ...), custom_call_target="tpu_custom_call" | custom-call | flops 7516192768 | bytes 88080384 | tf_op jit(solution)/shard_map/pallas_call | solution.py:52
  (27 shorter events, 0.4 us)
Async XLA Ops:
  7.2 36.6 %all-gather.3.cloned.1.call-start = ((), (), s32[]{:S(2)}) async-start(), calls=%async_computation.1 | async-start | bytes 4587520 | tf_op jit(solution)/shard_map/all_gather | solution.py:96
  7.9 139.0 %reduce-scatter.2.cloned.1.call-start = ((), (), s32[]{:S(2)}) async-start(), calls=%async_computation.2 | async-start | bytes 4718592 | tf_op jit(solution)/shard_map/reduce_scatter | solution.py:103
  8.0 47.9 %copy-start.1 = (bf16[128,2048]{1,0:T(8,128)(2,1)S(1)}, bf16[128,2048]{1,0:T(8,128)(2,1)}, u32[]{:S(2)}) copy-start(bf16[128,2048]{1,0:T(8,128)(2,1)} %param.10) | copy-start | bytes 1572868
  56.1 90.8 %copy-start.5 = (s32[4,2]{0,1:T(2,128)S(1)}, s32[4,2]{0,1:T(2,128)}, u32[]{:S(2)}) copy-start(s32[4,2]{0,1:T(2,128)} %param.16) | copy-start | bytes 100
  56.1 91.0 %copy-start.2 = (f32[2048]{0:T(1024)S(1)}, f32[2048]{0:T(1024)}, u32[]{:S(2)}) copy-start(f32[2048]{0:T(1024)} %param.14) | copy-start | bytes 24580
  56.1 91.0 %copy-start.3 = (f32[2048]{0:T(1024)S(1)}, f32[2048]{0:T(1024)}, u32[]{:S(2)}) copy-start(f32[2048]{0:T(1024)} %param.15) | copy-start | bytes 24580
  56.1 176.3 %copy-start.4 = (s32[4]{0:T(128)S(1)}, s32[4]{0:T(128)}, u32[]{:S(2)}) copy-start(s32[4]{0:T(128)} %param.17) | copy-start | bytes 52
  58.8 163.6 %all-gather.5.cloned.1.call-start = ((), (), s32[]{:S(2)}) async-start(), calls=%async_computation.3 | async-start | bytes 4718592 | tf_op jit(solution)/shard_map/all_gather | solution.py:104
  234.6 2.0 copy-start
Sparse Core Ops, SparseCore 0:
  9.6 34.1 all-gather.2
  58.9 87.8 reduce-scatter.1
  149.2 73.1 all-gather.4

commit v2 on v1

--- a/solution.py
+++ b/solution.py
@@ -11,6 +11,7 @@
 STEP = 100
 EPS_NORM = 1e-05
 MIB = 1024 * 1024
+MESH = pl.DeviceIdType.MESH
 
 
 def update_kernel(h_ref, s_ref, a_ref, b_ref, w_ref, p_ref, m_ref, v_ref, po_ref, mo_ref, vo_ref, cot):
@@ -90,18 +91,263 @@
     return a, b, loss
 
 
+def forward_kernel(dp, n, lanes, hidden, residual, master, hid_out, stream_out, hid, stream, partial,
+                   stage, weights, early_in, early_out, late_in, late_out, stage_sem, own_sem,
+                   block_send, block_recv, ring_send, ring_recv, out_sem):
+    f32, bf16 = jnp.float32, jnp.bfloat16
+    d, t = lax.axis_index("dp"), lax.axis_index("tensor")
+    pairs = dp // 2
+    q, core = d // 2, d % 2
+    rows, wide = hidden.shape[0], master.shape[1]
+    lane_cols, chunk = wide // lanes, rows // n
+    mate = 2 * q + 1 - core
+
+    def seat(place):
+        place = lax.rem(place + n, n)
+        return jnp.where(place < n // 2, 2 * place, 2 * (n - 1 - place) + 1)
+
+    place = jnp.where(t % 2 == 0, t // 2, n - 1 - t // 2)
+    right, left = seat(place + 1), seat(place - 1)
+
+    def block(k):
+        return 2 * lax.rem(q - k // 2 + pairs, pairs) + lax.rem(core + k, 2)
+
+    def block_rows(k):
+        return pl.ds(pl.multiple_of(block(k) * rows, rows), rows)
+
+    depth = stage_rows(master.shape[0])
+    pieces = master.shape[0] // depth
+
+    def stage_copy(i):
+        at = pl.ds(pl.multiple_of(i * depth, depth), depth)
+        return pltpu.make_async_copy(master.at[at], stage.at[at], stage_sem.at[i])
+
+    for i in range(pieces):
+        stage_copy(i).start()
+    own_copy = pltpu.make_async_copy(hidden, hid.at[block_rows(0)], own_sem)
+    own_copy.start()
+
+    barrier = pltpu.get_barrier_semaphore()
+    greeted = [{"tensor": right}, {"tensor": left}, {"dp": mate}]
+    greeted += [{"dp": 2 * lax.rem(q + j, pairs) + core} for j in range(1, pairs)]
+    for other in greeted:
+        pl.semaphore_signal(barrier, inc=1, device_id=other, device_id_type=MESH)
+    pl.semaphore_wait(barrier, len(greeted))
+
+    def block_copy(k):
+        if k == 1 or k % 2 == 0:
+            src, at = hidden, block_rows(0)
+        else:
+            src, at = hid.at[block_rows(k - 1)], block_rows(k - 1)
+        to = mate if k % 2 else 2 * lax.rem(q + k // 2, pairs) + core
+        return pltpu.make_async_remote_copy(
+            src_ref=src, dst_ref=hid.at[at], send_sem=block_send.at[k - 1], recv_sem=block_recv.at[k - 1],
+            device_id={"dp": to}, device_id_type=MESH,
+        )
+
+    def block_wait(k):
+        pltpu.make_async_remote_copy(
+            src_ref=hidden, dst_ref=hid.at[block_rows(k)], send_sem=block_send.at[k - 1],
+            recv_sem=block_recv.at[k - 1], device_id={"dp": mate}, device_id_type=MESH,
+        ).wait_recv()
+
+    for k in [1] + list(range(2, dp, 2)):
+        block_copy(k).start()
+
+    def to_weights(i, carry):
+        stage_copy(i).wait()
+        at = pl.ds(pl.multiple_of(i * depth, depth), depth)
+        weights[at, :] = stage[at, :].astype(bf16)
+        return carry
+
+    lax.fori_loop(0, pieces, to_weights, 0)
+
+    def multiply(k):
+        at = block_rows(k)
+
+        def tile(c, carry):
+            cols = pl.ds(pl.multiple_of(c * 256, 256), 256)
+            partial[k, :, cols] = jnp.dot(hid[at, :], weights[:, cols], preferred_element_type=f32)
+            return carry
+
+        lax.fori_loop(0, wide // 256, tile, 0)
+        res_rows = residual.shape[0]
+
+        @pl.when(block(k) == t * res_rows // rows)
+        def _():
+            own = pl.ds(pl.multiple_of(lax.rem(t * res_rows, rows), res_rows), res_rows)
+            partial[k, own, :] += residual[...].astype(f32)
+
+    sets = [(0, 0, 2, early_in, early_out), (1, 2, dp - 2, late_in, late_out)]
+
+    def chunk_at(lane, offset):
+        mirrored = place if lane % 2 == 0 else n - place
+        index = lax.rem(mirrored + offset + 2 * n, n)
+        return pl.ds(pl.multiple_of(index * chunk, chunk), chunk)
+
+    def ring_copy(which, lane, step, src, dst):
+        return pltpu.make_async_remote_copy(
+            src_ref=src, dst_ref=dst, send_sem=ring_send.at[which, lane, step],
+            recv_sem=ring_recv.at[which, lane, step],
+            device_id={"tensor": right if lane % 2 == 0 else left}, device_id_type=MESH,
+        )
+
+    def sum_copy(group, lane, step):
+        which, first, count, arrive, leave = group
+        return ring_copy(which, lane, step, leave.at[lane, step], arrive.at[lane, step])
+
+    def share_copy(group, lane, step, offset):
+        which, first, count, arrive, leave = group
+        at = stream.at[pl.ds(first, count), chunk_at(lane, offset), pl.ds(lane * lane_cols, lane_cols)]
+        return ring_copy(which, lane, n - 1 + step, at, at)
+
+    def own_part(group, lane, offset):
+        which, first, count, arrive, leave = group
+        return partial[pl.ds(first, count), chunk_at(lane, offset), pl.ds(lane * lane_cols, lane_cols)]
+
+    def begin(group):
+        for lane in range(lanes):
+            group[4][lane, 0] = own_part(group, lane, 0).astype(bf16)
+            sum_copy(group, lane, 0).start()
+
+    def add_step(group, step):
+        for lane in range(lanes):
+            sum_copy(group, lane, step - 1).wait_recv()
+            total = group[3][lane, step - 1].astype(f32) + own_part(group, lane, -step)
+            group[4][lane, step] = total.astype(bf16)
+            sum_copy(group, lane, step).start()
+
+    def turn(group):
+        which, first, count, arrive, leave = group
+        for lane in range(lanes):
+            sum_copy(group, lane, n - 2).wait_recv()
+            total = arrive[lane, n - 2].astype(f32) + own_part(group, lane, 1)
+            cols = pl.ds(lane * lane_cols, lane_cols)
+            stream[pl.ds(first, count), chunk_at(lane, 1), cols] = total.astype(bf16)
+            share_copy(group, lane, 0, 1).start()
+
+    def share_step(group, step):
+        for lane in range(lanes):
+            share_copy(group, lane, step - 1, 1 - step).wait_recv()
+            share_copy(group, lane, step, 1 - step).start()
+
+    def finish(group):
+        for lane in range(lanes):
+            share_copy(group, lane, n - 2, 2 - n).wait_recv()
+
+    def sent(group):
+        for lane in range(lanes):
+
+            def wait(step, carry):
+                sum_copy(group, lane, step).wait_send()
+                share_copy(group, lane, step, 1 - step).wait_send()
+                return carry
+
+            lax.fori_loop(0, n - 1, wait, 0)
+
+    def result_copy(k):
+        return pltpu.make_async_copy(stream.at[k], stream_out.at[block_rows(k)], out_sem.at[k])
+
+    early, late = sets
+    own_copy.wait()
+    multiply(0)
+    block_wait(1)
+    multiply(1)
+    begin(early)
+
+    def early_sums(step, carry):
+        add_step(early, step)
+        return carry
+
+    lax.fori_loop(1, n - 1, early_sums, 0)
+    turn(early)
+    for k in range(2, dp, 2):
+        block_wait(k)
+        block_copy(k + 1).start()
+    for k in range(2, dp):
+        if k % 2:
+            block_wait(k)
+        multiply(k)
+    hid_copy = pltpu.make_async_copy(hid, hid_out, out_sem.at[dp])
+    hid_copy.start()
+    begin(late)
+
+    def both(step, carry):
+        share_step(early, step)
+        add_step(late, step)
+        return carry
+
+    lax.fori_loop(1, n - 1, both, 0)
+    finish(early)
+    turn(late)
+    for k in range(2):
+        result_copy(k).start()
+
+    def late_shares(step, carry):
+        share_step(late, step)
+        return carry
+
+    lax.fori_loop(1, n - 1, late_shares, 0)
+    finish(late)
+    for k in range(2, dp):
+        result_copy(k).start()
+    for k in range(1, dp):
+        block_copy(k).wait_send()
+    sent(early)
+    sent(late)
+    for k in range(dp):
+        result_copy(k).wait()
+    hid_copy.wait()
+
+
+def stage_rows(depth):
+    return 128 if depth % 128 == 0 else depth
+
+
+def forward(dp, n, hidden, residual, master):
+    rows, depth = hidden.shape
+    wide = master.shape[1]
+    tokens = rows * dp
+    lanes = 4
+    chunk, lane_cols = rows // n, wide // lanes
+    bf16 = jnp.bfloat16
+    slots = lambda count: pltpu.VMEM((lanes, n - 1, count, chunk, lane_cols), bf16)
+    dma = pltpu.SemaphoreType.DMA
+    vmem = pl.BlockSpec(memory_space=pltpu.VMEM)
+    hbm = pl.BlockSpec(memory_space=pl.ANY)
+    return pl.pallas_call(
+        functools.partial(forward_kernel, dp, n, lanes),
+        in_specs=[vmem, vmem, hbm],
+        out_specs=[hbm, hbm],
+        out_shape=[
+            jax.ShapeDtypeStruct((tokens, depth), bf16),
+            jax.ShapeDtypeStruct((tokens, wide), bf16),
+        ],
+        scratch_shapes=[
+            pltpu.VMEM((tokens, depth), bf16),
+            pltpu.VMEM((dp, rows, wide), bf16),
+            pltpu.VMEM((dp, rows, wide), jnp.float32),
+            pltpu.VMEM((depth, wide), jnp.float32),
+            pltpu.VMEM((depth, wide), bf16),
+            slots(2), slots(2), slots(dp - 2), slots(dp - 2),
+            dma((depth // stage_rows(depth),)),
+            dma,
+            dma((dp - 1,)), dma((dp - 1,)),
+            dma((2, lanes, 2 * n - 2)), dma((2, lanes, 2 * n - 2)),
+            dma((dp + 1,)),
+        ],
+        compiler_params=pltpu.CompilerParams(
+            collective_id=0, has_side_effects=True, vmem_limit_bytes=60 * MIB
+        ),
+        cost_estimate=pl.CostEstimate(
+            flops=2 * tokens * depth * wide, bytes_accessed=4 * depth * wide + 4 * tokens * depth,
+            transcendentals=0,
+        ),
+    )(hidden, residual, master)
+
+
 def per_device(dp, tensor, hidden, residual, master, moment, second, gain, head, lengths, labels):
-    t_index = lax.axis_index("tensor")
-    block_rows = residual.shape[0]
-    gathered = lax.all_gather(hidden, "dp", axis=0, tiled=True)
-    partial_value = jnp.dot(gathered, master.astype(jnp.bfloat16), preferred_element_type=jnp.float32)
-    row_start = t_index * block_rows
-    own = lax.dynamic_slice_in_dim(partial_value, row_start, block_rows, 0) + residual.astype(
-        jnp.float32
-    )
-    term = lax.dynamic_update_slice_in_dim(partial_value, own, row_start, 0).astype(jnp.bfloat16)
-    part = lax.psum_scatter(term, "tensor", scatter_dimension=0, tiled=True)
-    stream = lax.all_gather(part, "tensor", axis=0, tiled=True)
+    gathered, stream = forward(dp, tensor, hidden, residual, master)
     w = gain * head
     a, b, loss = row_terms(stream, w, lengths, labels, w.shape[0] * dp)
     new_master, new_moment, new_second = update(

time: 286 us -> 178 us (0.62)
  waiting for transfers between devices: 200 us -> 0 us
  Pallas kernels: 43.1 us -> 161 us
  between operations: 13.9 us -> 0.76 us
  matrix products: 12.1 us -> 0 us
    pallas_call x0 -> x1, Pallas kernels: none -> 118 us  [forward(): pl.pallas_call(functools.partial(forward_kernel, dp, n, lanes), in_specs=...]
    all_gather x2 -> x0, waiting for transfers between devices: 111 us -> none  [the longest x1 75.3 us: per_device(): stream = lax.all_gather(part, 'tensor', axis=0, tiled=True)]
    reduce_scatter x1 -> x0, waiting for transfers between devices: 88 us -> none  [per_device(): part = lax.psum_scatter(term, 'tensor', scatter_dimension=0, tiled=True)]
    dot_general x1 -> x0, matrix products: 12.1 us -> none  [per_device(): jnp.dot(gathered, master.astype(jnp.bfloat16), preferred_element_type=jnp...]
  transfers between devices with their start and end apart: 3 -> 0, of which waited for: 3 -> 0; matrix products, arithmetic and copies ran while one was open for 0% -> 0% of each run, Pallas kernels for 0% -> 0%
where the time goes in v2:
time: 178 us
  Pallas kernels  161 us (90%)
  blocking collectives  5.77 us (3%)
  other arithmetic  5.44 us (3%)
  local copies, waits for them, and re-layouts  4.47 us (3%)
    pallas_call x1, Pallas kernels, forward(): pl.pallas_call(functools.partial(forward_kernel, dp, n, lanes), in_specs=...  118 us
    pallas_call x1, Pallas kernels, update(): pl.pallas_call(update_kernel, grid=(ff // tile,), in_specs=[pl.BlockSpec(...  43.1 us
    psum x1, blocking collectives, row_terms(): squares, product = lax.psum(sums, 'dp')  5.77 us
    reduce_sum x1, other arithmetic, row_terms(): jnp.sum(value * value, 1)  3.66 us

profile of v2, /device:TPU:0, one launch (start us, length us, event | category | flops | bytes accessed | tf_op | source)
XLA Modules:
  0.0 177.8 jit_solution(6928058668043303187)
XLA Ops:
  0.6 0.8 copy.26
  1.4 0.1 lt.32
  1.5 0.7 mul.55
  2.2 0.0 copy-start.1
  2.2 118.3 %shard_map.120 = (bf16[1024,1792]{1,0:T(8,128)(2,1)}, bf16[1024,2048]{1,0:T(8,128)(2,1)}) custom-call(bf16[256,1792]{1,0:T(8,128)(2,1)} %hidden.1, bf16[128,2048]{1,0:T(8,128)(2,1)} %residual.1, f32[1792,2048]{1,0:T(8,128)} %p_ref.1), custom_call_target="tpu_custom_call" | custom-call | flops 7516192768 | bytes 22020096 | tf_op jit(solution)/shard_map/pallas_call | solution.py:318
  120.5 3.7 %fusion = (f32[1024]{0:T(1024)S(1)}, f32[1024]{0:T(1024)S(1)}) fusion(bf16[1024,2048]{1,0:T(8,128)(2,1)} %get-tuple-element.10.s_ref, f32[2048]{0:T(1024)S(1)} %mul.55), kind=kLoop, calls=%fused_computation.2 | loop fusion | flops 10483712 | bytes 4210688 | tf_op jit(solution)/shard_map/reduce_sum | solution.py:71
  124.1 5.8 %psum.7 = f32[2,1024]{1,0:T(2,128)S(1)} all-reduce(f32[2,1024]{1,0:T(2,128)S(1)} %pad_maximum_fusion), channel_id=1, replica_groups=mesh['dp'=4,'tensor'=8] {'dp'}, use_global_device_ids=true, to_apply=%region_2.0 | all-reduce | flops 2048 | bytes 16384 | tf_op jit(solution)/shard_map/psum | solution.py:72
  130.0 0.2 select_reduce_fusion
  130.1 0.1 reduce_sum.41
  130.2 0.2 slice_reduce_fusion
  130.4 0.0 copy-done.1
  130.4 0.6 fusion.6
  131.1 0.1 copy.28
  131.2 0.1 reshape.148
  131.3 0.1 fusion.4
  131.4 0.2 copy.32
  131.6 0.2 copy.33.a_ref
  131.8 0.2 copy.31
  132.1 0.2 copy.29
  132.3 0.2 copy.30
  132.5 0.1 multiply_multiply_fusion.b_ref
  132.6 0.0 copy-start
  132.7 2.0 %copy-done = bf16[1024,1792]{1,0:T(8,128)(2,1)S(1)} copy-done((bf16[1024,1792]{1,0:T(8,128)(2,1)S(1)}, bf16[1024,1792]{1,0:T(8,128)(2,1)}, u32[]{:S(2)}) %copy-start) | copy-done | bytes 3670040
  134.7 43.1 %shard_map.121 = (f32[1792,2048]{1,0:T(8,128)}, f32[1792,2048]{1,0:T(8,128)}, f32[1792,2048]{1,0:T(8,128)}) custom-call(bf16[1024,1792]{1,0:T(8,128)(2,1)S(1)} %copy-done, bf16[1024,2048]{1,0:T(8,128)(2,1)} %get-tuple-element.10.s_ref, f32[1024,1]{1,0:T(8,128)S(1)} %copy.33.a_ref, f32[1024,1]{1,0:T(8,128)S(1)} %multiply_multiply_fusion.b_ref, ...), custom_call_target="tpu_custom_call" | custom-call | flops 7516192768 | bytes 88080384 | tf_op jit(solution)/shard_map/pallas_call | solution.py:53
  (8 shorter events, 0.1 us)
Async XLA Ops:
  2.2 128.2 %copy-start.1 = (s32[4]{0:T(128)S(1)}, s32[4]{0:T(128)}, u32[]{:S(2)}) copy-start(s32[4]{0:T(128)} %param.17) | copy-start | bytes 52
  132.6 2.0 %copy-start = (bf16[1024,1792]{1,0:T(8,128)(2,1)S(1)}, bf16[1024,1792]{1,0:T(8,128)(2,1)}, u32[]{:S(2)}) copy-start(bf16[1024,1792]{1,0:T(8,128)(2,1)} %get-tuple-element.9.h_ref) | copy-start | bytes 11010052

commit v3 on v2

--- a/solution.py
+++ b/solution.py
@@ -14,67 +14,69 @@
 MESH = pl.DeviceIdType.MESH
 
 
-def update_kernel(h_ref, s_ref, a_ref, b_ref, w_ref, p_ref, m_ref, v_ref, po_ref, mo_ref, vo_ref, cot):
-    @pl.when(pl.program_id(0) == 0)
+def update_kernel(ht_ref, s_ref, a_ref, b_ref, w_ref, p_ref, m_ref, v_ref, po_ref, mo_ref, vo_ref, cot):
+    tile = p_ref.shape[0]
+
+    @pl.when(pl.program_id(1) == 0)
     def _():
-        def fill(i, carry):
-            rows = pl.ds(pl.multiple_of(i * 64, 64), 64)
-            value = a_ref[rows, :] * w_ref[...] - b_ref[rows, :] * s_ref[rows, :].astype(jnp.float32)
+        a, b = a_ref[...].T, b_ref[...].T
+        for seq in range(a.shape[1]):
+            rows = slice(seq * LEN, (seq + 1) * LEN)
+            value = a[:, seq : seq + 1] * w_ref[...] - b[:, seq : seq + 1] * s_ref[rows, :].astype(
+                jnp.float32
+            )
             cot[rows, :] = value.astype(jnp.bfloat16)
-            return carry
-
-        lax.fori_loop(0, cot.shape[0] // 64, fill, 0)
-
-    h = h_ref[...]
-    wide = cot.shape[1]
-    step = 512
-    for c in range(wide // step):
-        cols = slice(c * step, (c + 1) * step)
-        grad = lax.dot_general(
-            h, cot[:, cols], (((0,), (0,)), ((), ())), preferred_element_type=jnp.float32
-        )
-        moment = 0.9 * m_ref[:, cols] + 0.1 * grad
-        second = 0.95 * v_ref[:, cols] + 0.05 * grad * grad
-        mo_ref[:, cols] = moment
-        vo_ref[:, cols] = second
+
+    start = pl.program_id(1) * tile
+    part = 128
+
+    def step(i, carry):
+        rows = pl.ds(pl.multiple_of(i * part, part), part)
+        at = pl.ds(pl.multiple_of(start + i * part, part), part)
+        grad = jnp.dot(ht_ref[at, :], cot[...], preferred_element_type=jnp.float32)
+        moment = 0.9 * m_ref[rows, :] + 0.1 * grad
+        second = 0.95 * v_ref[rows, :] + 0.05 * grad * grad
+        mo_ref[rows, :] = moment
+        vo_ref[rows, :] = second
         m_hat = moment * (1.0 / (1.0 - 0.9**STEP))
         v_hat = second * (1.0 / (1.0 - 0.95**STEP))
-        master = p_ref[:, cols]
-        po_ref[:, cols] = master - 0.001 * (m_hat / (jnp.sqrt(v_hat) + 1e-08) + 0.1 * master)
-
-
-def update(hidden, stream, a, b, w, master, moment, second):
-    tokens, ff = hidden.shape
+        master = p_ref[rows, :]
+        po_ref[rows, :] = master - 0.001 * (m_hat / (jnp.sqrt(v_hat) + 1e-08) + 0.1 * master)
+        return carry
+
+    for i in range(tile // part):
+        step(i, 0)
+
+
+def update(ht, stream, a, b, w, master, moment, second):
+    ff, tokens = ht.shape
     wide = stream.shape[1]
-    tile = 128
-    state = pl.BlockSpec((tile, wide), lambda i: (i, 0))
-    whole = lambda x: pl.BlockSpec(x.shape, lambda i: (0, 0), pipeline_mode=pl.Buffered(1))
+    tile, cols = ff // 2, 256
+    state = pl.BlockSpec((tile, cols), lambda j, i: (i, j))
+    whole = lambda x: pl.BlockSpec(x.shape, lambda j, i: (0, 0), pipeline_mode=pl.Buffered(1))
     out = jax.ShapeDtypeStruct(master.shape, jnp.float32)
     return pl.pallas_call(
         update_kernel,
-        grid=(ff // tile,),
-        in_specs=[pl.BlockSpec((tokens, tile), lambda i: (0, i))]
-        + [whole(x) for x in (stream, a, b, w)]
+        grid=(wide // cols, ff // tile),
+        in_specs=[
+            whole(ht), pl.BlockSpec((tokens, cols), lambda j, i: (0, j)), whole(a), whole(b),
+            pl.BlockSpec((1, cols), lambda j, i: (0, j)),
+        ]
         + [state] * 3,
         out_specs=[state] * 3,
         out_shape=[out] * 3,
-        scratch_shapes=[pltpu.VMEM(stream.shape, jnp.bfloat16)],
+        scratch_shapes=[pltpu.VMEM((tokens, cols), jnp.bfloat16)],
         compiler_params=pltpu.CompilerParams(vmem_limit_bytes=48 * MIB),
         cost_estimate=pl.CostEstimate(
             flops=2 * tokens * ff * wide, bytes_accessed=24 * ff * wide, transcendentals=ff * wide
         ),
-    )(hidden, stream, a, b, w, master, moment, second)
-
-
-def row_terms(stream, w, lengths, labels, full_width):
-    value = stream.astype(jnp.float32)
-    sums = jnp.stack([jnp.sum(value * value, 1), jnp.sum(value * w[None, :], 1)])
-    squares, product = lax.psum(sums, "dp")
+    )(ht, stream, a, b, w, master, moment, second)
+
+
+def row_terms(squares, product, lengths, labels, full_width):
     lens = lengths.reshape(-1)
     lens_f = lens.astype(jnp.float32)[:, None]
     valid = jnp.arange(LEN, dtype=jnp.int32)[None, :] < lens[:, None]
-    squares = squares.reshape(-1, LEN)
-    product = product.reshape(-1, LEN)
     rstd = lax.rsqrt(squares / full_width + EPS_NORM)
     total = jnp.sum(jnp.where(valid, rstd * product, 0.0), 1)
     reward = (total / lens_f[:, 0]).reshape(-1, 2)
@@ -86,14 +88,14 @@
     first = jnp.where(labels == 0, -sig, sig)
     dreward = jnp.stack([first, -first], 1).reshape(-1, 1)
     coef = jnp.where(valid, dreward / lens_f, 0.0)
-    a = (coef * rstd).reshape(-1, 1)
-    b = (coef * (product * rstd**3 / full_width)).reshape(-1, 1)
+    a = coef * rstd
+    b = coef * (product * rstd**3 / full_width)
     return a, b, loss
 
 
-def forward_kernel(dp, n, lanes, hidden, residual, master, hid_out, stream_out, hid, stream, partial,
-                   stage, weights, early_in, early_out, late_in, late_out, stage_sem, own_sem,
-                   block_send, block_recv, ring_send, ring_recv, out_sem):
+def forward_kernel(dp, n, lanes, hidden, residual, w, master, hid_out, stream_out, sums_out, hid, hid_t,
+                   stream, partial, sums, stage, weights, early_in, early_out, late_in, late_out, stage_sem, own_sem,
+                   block_send, block_recv, ring_send, ring_recv, sums_send, sums_recv, out_sem):
     f32, bf16 = jnp.float32, jnp.bfloat16
     d, t = lax.axis_index("dp"), lax.axis_index("tensor")
     pairs = dp // 2
@@ -128,8 +130,8 @@
     own_copy.start()
 
     barrier = pltpu.get_barrier_semaphore()
-    greeted = [{"tensor": right}, {"tensor": left}, {"dp": mate}]
-    greeted += [{"dp": 2 * lax.rem(q + j, pairs) + core} for j in range(1, pairs)]
+    greeted = [{"tensor": right}, {"tensor": left}]
+    greeted += [{"dp": lax.rem(d + j, dp)} for j in range(1, dp)]
     for other in greeted:
         pl.semaphore_signal(barrier, inc=1, device_id=other, device_id_type=MESH)
     pl.semaphore_wait(barrier, len(greeted))
@@ -248,6 +250,34 @@
     def result_copy(k):
         return pltpu.make_async_copy(stream.at[k], stream_out.at[block_rows(k)], out_sem.at[k])
 
+    def block_sums(k):
+        for seq in range(rows // LEN):
+            at = slice(seq * LEN, (seq + 1) * LEN)
+            squares = jnp.zeros((LEN, 128), f32)
+            product = jnp.zeros((LEN, 128), f32)
+            for c in range(wide // 128):
+                cols = slice(c * 128, (c + 1) * 128)
+                value = stream[k, at, cols].astype(f32)
+                squares += value * value
+                product += value * w[:, cols]
+            sums[d, block(k), 0, seq : seq + 1, :] = jnp.sum(squares.T, 0, keepdims=True)
+            sums[d, block(k), 1, seq : seq + 1, :] = jnp.sum(product.T, 0, keepdims=True)
+
+    def sums_copy(j, source):
+        return pltpu.make_async_remote_copy(
+            src_ref=sums.at[d], dst_ref=sums.at[source], send_sem=sums_send.at[j - 1],
+            recv_sem=sums_recv.at[j - 1], device_id={"dp": lax.rem(d + j, dp)}, device_id_type=MESH,
+        )
+
+    units = hid.shape[1] // 128
+    per_step = -(-units // (n - 2))
+
+    def turn_unit(i):
+        @pl.when(i < units)
+        def _():
+            cols = pl.ds(pl.multiple_of(i * 128, 128), 128)
+            hid_t[cols, :] = hid[:, cols].T
+
     early, late = sets
     own_copy.wait()
     multiply(0)
@@ -268,20 +298,23 @@
         if k % 2:
             block_wait(k)
         multiply(k)
-    hid_copy = pltpu.make_async_copy(hid, hid_out, out_sem.at[dp])
-    hid_copy.start()
+    hid_copy = pltpu.make_async_copy(hid_t, hid_out, out_sem.at[dp])
     begin(late)
 
     def both(step, carry):
         share_step(early, step)
         add_step(late, step)
+        for j in range(per_step):
+            turn_unit((step - 1) * per_step + j)
         return carry
 
     lax.fori_loop(1, n - 1, both, 0)
     finish(early)
     turn(late)
+    hid_copy.start()
     for k in range(2):
         result_copy(k).start()
+        block_sums(k)
 
     def late_shares(step, carry):
         share_step(late, step)
@@ -291,10 +324,21 @@
     finish(late)
     for k in range(2, dp):
         result_copy(k).start()
+        block_sums(k)
+    for j in range(1, dp):
+        sums_copy(j, d).start()
     for k in range(1, dp):
         block_copy(k).wait_send()
     sent(early)
     sent(late)
+    for j in range(1, dp):
+        sums_copy(j, lax.rem(d - j + dp, dp)).wait_recv()
+    total = sums[0]
+    for source in range(1, dp):
+        total += sums[source]
+    sums_out[...] = total
+    for j in range(1, dp):
+        sums_copy(j, d).wait_send()
     for k in range(dp):
         result_copy(k).wait()
     hid_copy.wait()
@@ -304,7 +348,7 @@
     return 128 if depth % 128 == 0 else depth
 
 
-def forward(dp, n, hidden, residual, master):
+def forward(dp, n, hidden, residual, w, master):
     rows, depth = hidden.shape
     wide = master.shape[1]
     tokens = rows * dp
@@ -317,16 +361,19 @@
     hbm = pl.BlockSpec(memory_space=pl.ANY)
     return pl.pallas_call(
         functools.partial(forward_kernel, dp, n, lanes),
-        in_specs=[vmem, vmem, hbm],
-        out_specs=[hbm, hbm],
+        in_specs=[vmem, vmem, vmem, hbm],
+        out_specs=[hbm, hbm, vmem],
         out_shape=[
-            jax.ShapeDtypeStruct((tokens, depth), bf16),
+            jax.ShapeDtypeStruct((depth, tokens), bf16),
             jax.ShapeDtypeStruct((tokens, wide), bf16),
+            jax.ShapeDtypeStruct((dp, 2, rows // LEN, LEN), jnp.float32),
         ],
         scratch_shapes=[
             pltpu.VMEM((tokens, depth), bf16),
+            pltpu.VMEM((depth, tokens), bf16),
             pltpu.VMEM((dp, rows, wide), bf16),
             pltpu.VMEM((dp, rows, wide), jnp.float32),
+            pltpu.VMEM((dp, dp, 2, rows // LEN, LEN), jnp.float32),
             pltpu.VMEM((depth, wide), jnp.float32),
             pltpu.VMEM((depth, wide), bf16),
             slots(2), slots(2), slots(dp - 2), slots(dp - 2),
@@ -334,6 +381,7 @@
             dma,
             dma((dp - 1,)), dma((dp - 1,)),
             dma((2, lanes, 2 * n - 2)), dma((2, lanes, 2 * n - 2)),
+            dma((dp - 1,)), dma((dp - 1,)),
             dma((dp + 1,)),
         ],
         compiler_params=pltpu.CompilerParams(
@@ -343,15 +391,16 @@
             flops=2 * tokens * depth * wide, bytes_accessed=4 * depth * wide + 4 * tokens * depth,
             transcendentals=0,
         ),
-    )(hidden, residual, master)
+    )(hidden, residual, w, master)
 
 
 def per_device(dp, tensor, hidden, residual, master, moment, second, gain, head, lengths, labels):
-    gathered, stream = forward(dp, tensor, hidden, residual, master)
-    w = gain * head
-    a, b, loss = row_terms(stream, w, lengths, labels, w.shape[0] * dp)
+    w = (gain * head)[None, :]
+    hidden_t, stream, sums = forward(dp, tensor, hidden, residual, w, master)
+    squares, product = sums[:, 0].reshape(-1, LEN), sums[:, 1].reshape(-1, LEN)
+    a, b, loss = row_terms(squares, product, lengths, labels, w.shape[1] * dp)
     new_master, new_moment, new_second = update(
-        gathered, stream, a, b, w[None, :], master, moment, second
+        hidden_t, stream, a, b, w, master, moment, second
     )
     return new_master, new_moment, new_second, loss
 

time: 178 us -> 175 us (0.983)
  Pallas kernels: 161 us -> 168 us
  blocking collectives: 5.77 us -> 0 us
  other arithmetic: 5.44 us -> 2.89 us
    psum x1 -> x0, blocking collectives: 5.77 us -> none  [row_terms(): squares, product = lax.psum(sums, 'dp')]
    reduce_sum x2 -> x0, other arithmetic: 3.85 us -> none  [the longest x1 3.66 us: row_terms(): jnp.sum(value * value, 1)]
    pallas_call x1, Pallas kernels: 118 us -> 122 us  [forward(): pl.pallas_call(functools.partial(forward_kernel, dp, n, lanes), in_specs=...]
    pallas_call x1, Pallas kernels: 43.1 us -> 45.9 us  [update(): pl.pallas_call(update_kernel, grid=(wide // cols, ff // tile), in_specs=[...]
where the time goes in v3:
time: 175 us
  Pallas kernels  168 us (96%)
  local copies, waits for them, and re-layouts  3.28 us (2%)
  other arithmetic  2.89 us (2%)
    pallas_call x1, Pallas kernels, forward(): pl.pallas_call(functools.partial(forward_kernel, dp, n, lanes), in_specs=...  122 us
    pallas_call x1, Pallas kernels, update(): pl.pallas_call(update_kernel, grid=(wide // cols, ff // tile), in_specs=[...  45.9 us

profile of v3, /device:TPU:0, one launch (start us, length us, event | category | flops | bytes accessed | tf_op | source)
XLA Modules:
  0.0 174.6 jit_solution(8122427542017764068)
XLA Ops:
  0.6 0.0 copy-start.2
  0.6 0.8 copy.23
  1.4 0.1 lt.29
  1.5 1.3 mul.16
  2.8 0.0 copy-start.1
  2.8 121.9 %shard_map.120 = (bf16[1792,1024]{1,0:T(8,128)(2,1)}, bf16[1024,2048]{1,0:T(8,128)(2,1)}, f32[4,2,2,128]{3,2,1,0:T(2,128)}) custom-call(bf16[256,1792]{1,0:T(8,128)(2,1)} %hidden.1, bf16[128,2048]{1,0:T(8,128)(2,1)} %residual.1, f32[1,2048]{1,0:T(1,128)} %bitcast.6, f32[1792,2048]{1,0:T(8,128)} %p_ref.1), custom_call_target="tpu_custom_call" | custom-call | flops 7516192768 | bytes 22020096 | tf_op jit(solution)/shard_map/pallas_call | solution.py:362
  124.7 0.8 fusion.6
  125.5 0.2 slice_reduce_fusion
  125.7 0.0 copy-done.2
  125.7 0.6 fusion.4
  126.4 0.1 copy.26
  126.5 0.1 reshape.50
  126.6 0.1 select_multiply_fusion
  126.7 0.0 copy-done.1
  126.7 0.0 copy-start
  126.7 2.0 %copy-done = bf16[1792,1024]{1,0:T(8,128)(2,1)S(1)} copy-done((bf16[1792,1024]{1,0:T(8,128)(2,1)S(1)}, bf16[1792,1024]{1,0:T(8,128)(2,1)}, u32[]{:S(2)}) %copy-start) | copy-done | bytes 3670040
  128.7 45.9 %shard_map.121 = (f32[1792,2048]{1,0:T(8,128)}, f32[1792,2048]{1,0:T(8,128)}, f32[1792,2048]{1,0:T(8,128)}) custom-call(bf16[1792,1024]{1,0:T(8,128)(2,1)S(1)} %copy-done, bf16[1024,2048]{1,0:T(8,128)(2,1)} %get-tuple-element.11.s_ref, f32[8,128]{1,0:T(8,128)S(1)} %get-tuple-element.26.a_ref, f32[8,128]{1,0:T(8,128)S(1)} %get-tuple-element.25.b_ref, ...), custom_call_target="tpu_custom_call" | custom-call | flops 7516192768 | bytes 88080384 | tf_op jit(solution)/shard_map/pallas_call | solution.py:58
  (4 shorter events, 0.0 us)
Async XLA Ops:
  0.6 125.1 %copy-start.2 = (s32[4]{0:T(128)S(1)}, s32[4]{0:T(128)}, u32[]{:S(2)}) copy-start(s32[4]{0:T(128)} %param.17) | copy-start | bytes 52
  2.8 123.8 %copy-start.1 = (f32[2048]{0:T(1024)S(1)}, f32[2048]{0:T(1024)}, u32[]{:S(2)}) copy-start(f32[2048]{0:T(1024)} %mul.16) | copy-start | bytes 24580
  126.7 2.1 %copy-start = (bf16[1792,1024]{1,0:T(8,128)(2,1)S(1)}, bf16[1792,1024]{1,0:T(8,128)(2,1)}, u32[]{:S(2)}) copy-start(bf16[1792,1024]{1,0:T(8,128)(2,1)} %get-tuple-element.10.ht_ref) | copy-start | bytes 11010052

commit v4 on v3

--- a/solution.py
+++ b/solution.py
@@ -66,7 +66,7 @@
         out_specs=[state] * 3,
         out_shape=[out] * 3,
         scratch_shapes=[pltpu.VMEM((tokens, cols), jnp.bfloat16)],
-        compiler_params=pltpu.CompilerParams(vmem_limit_bytes=48 * MIB),
+        compiler_params=pltpu.CompilerParams(vmem_limit_bytes=20 * MIB),
         cost_estimate=pl.CostEstimate(
             flops=2 * tokens * ff * wide, bytes_accessed=24 * ff * wide, transcendentals=ff * wide
         ),
@@ -122,9 +122,11 @@
 
     def stage_copy(i):
         at = pl.ds(pl.multiple_of(i * depth, depth), depth)
-        return pltpu.make_async_copy(master.at[at], stage.at[at], stage_sem.at[i])
-
-    for i in range(pieces):
+        slot = lax.rem(i, slots)
+        return pltpu.make_async_copy(master.at[at], stage.at[slot], stage_sem.at[slot])
+
+    slots = stage.shape[0]
+    for i in range(slots):
         stage_copy(i).start()
     own_copy = pltpu.make_async_copy(hidden, hid.at[block_rows(0)], own_sem)
     own_copy.start()
@@ -159,26 +161,40 @@
     def to_weights(i, carry):
         stage_copy(i).wait()
         at = pl.ds(pl.multiple_of(i * depth, depth), depth)
-        weights[at, :] = stage[at, :].astype(bf16)
+        weights[at, :] = stage[lax.rem(i, slots)].astype(bf16)
+
+        @pl.when(i + slots < pieces)
+        def _():
+            stage_copy(i + slots).start()
+
         return carry
 
     lax.fori_loop(0, pieces, to_weights, 0)
 
-    def multiply(k):
-        at = block_rows(k)
-
-        def tile(c, carry):
-            cols = pl.ds(pl.multiple_of(c * 256, 256), 256)
-            partial[k, :, cols] = jnp.dot(hid[at, :], weights[:, cols], preferred_element_type=f32)
-            return carry
-
-        lax.fori_loop(0, wide // 256, tile, 0)
+    tiles = wide // 256
+
+    def multiply_tile(k, c):
+        cols = pl.ds(pl.multiple_of(c * 256, 256), 256)
+        partial[k, :, cols] = jnp.dot(
+            hid[block_rows(k), :], weights[:, cols], preferred_element_type=f32
+        ).astype(bf16)
+
+    def add_residual(k):
         res_rows = residual.shape[0]
 
         @pl.when(block(k) == t * res_rows // rows)
         def _():
             own = pl.ds(pl.multiple_of(lax.rem(t * res_rows, rows), res_rows), res_rows)
-            partial[k, own, :] += residual[...].astype(f32)
+            total = partial[k, own, :].astype(f32) + residual[...].astype(f32)
+            partial[k, own, :] = total.astype(bf16)
+
+    def multiply(k):
+        def tile(c, carry):
+            multiply_tile(k, c)
+            return carry
+
+        lax.fori_loop(0, tiles, tile, 0)
+        add_residual(k)
 
     sets = [(0, 0, 2, early_in, early_out), (1, 2, dp - 2, late_in, late_out)]
 
@@ -196,7 +212,13 @@
 
     def sum_copy(group, lane, step):
         which, first, count, arrive, leave = group
-        return ring_copy(which, lane, step, leave.at[lane, step], arrive.at[lane, step])
+        src = leave.at[lane] if step is None else arrive.at[lane, step - 1]
+        at = 0 if step is None else step
+        return ring_copy(which, lane, at, src, arrive.at[lane, at])
+
+    def arrival(group, lane, step):
+        which, first, count, arrive, leave = group
+        return ring_copy(which, lane, step, leave.at[lane], arrive.at[lane, step])
 
     def share_copy(group, lane, step, offset):
         which, first, count, arrive, leave = group
@@ -209,21 +231,21 @@
 
     def begin(group):
         for lane in range(lanes):
-            group[4][lane, 0] = own_part(group, lane, 0).astype(bf16)
-            sum_copy(group, lane, 0).start()
+            group[4][lane] = own_part(group, lane, 0)
+            sum_copy(group, lane, None).start()
 
     def add_step(group, step):
         for lane in range(lanes):
-            sum_copy(group, lane, step - 1).wait_recv()
-            total = group[3][lane, step - 1].astype(f32) + own_part(group, lane, -step)
-            group[4][lane, step] = total.astype(bf16)
+            arrival(group, lane, step - 1).wait_recv()
+            total = group[3][lane, step - 1].astype(f32) + own_part(group, lane, -step).astype(f32)
+            group[3][lane, step - 1] = total.astype(bf16)
             sum_copy(group, lane, step).start()
 
     def turn(group):
         which, first, count, arrive, leave = group
         for lane in range(lanes):
-            sum_copy(group, lane, n - 2).wait_recv()
-            total = arrive[lane, n - 2].astype(f32) + own_part(group, lane, 1)
+            arrival(group, lane, n - 2).wait_recv()
+            total = arrive[lane, n - 2].astype(f32) + own_part(group, lane, 1).astype(f32)
             cols = pl.ds(lane * lane_cols, lane_cols)
             stream[pl.ds(first, count), chunk_at(lane, 1), cols] = total.astype(bf16)
             share_copy(group, lane, 0, 1).start()
@@ -241,7 +263,7 @@
         for lane in range(lanes):
 
             def wait(step, carry):
-                sum_copy(group, lane, step).wait_send()
+                arrival(group, lane, step).wait_send()
                 share_copy(group, lane, step, 1 - step).wait_send()
                 return carry
 
@@ -289,15 +311,35 @@
         add_step(early, step)
         return carry
 
-    lax.fori_loop(1, n - 1, early_sums, 0)
-    turn(early)
+    def early_sums_and_tiles(step, carry):
+        add_step(early, step)
+
+        def tile(j, inner):
+            i = (step - middle) * tiles_per_step + j
+
+            @pl.when(i < late_tiles)
+            def _():
+                multiply_tile(2 + i // tiles, lax.rem(i, tiles))
+
+            return inner
+
+        lax.fori_loop(0, tiles_per_step, tile, 0)
+        return carry
+
+    first, middle = (n - 1) // 3, (n - 1) // 3 + 2
+    late_tiles = (dp - 2) * tiles
+    tiles_per_step = -(-late_tiles // (n - 1 - middle))
+    lax.fori_loop(1, first + 1, early_sums, 0)
     for k in range(2, dp, 2):
         block_wait(k)
         block_copy(k + 1).start()
+    lax.fori_loop(first + 1, middle, early_sums, 0)
+    for k in range(3, dp, 2):
+        block_wait(k)
+    lax.fori_loop(middle, n - 1, early_sums_and_tiles, 0)
+    turn(early)
     for k in range(2, dp):
-        if k % 2:
-            block_wait(k)
-        multiply(k)
+        add_residual(k)
     hid_copy = pltpu.make_async_copy(hid_t, hid_out, out_sem.at[dp])
     begin(late)
 
@@ -356,6 +398,7 @@
     chunk, lane_cols = rows // n, wide // lanes
     bf16 = jnp.bfloat16
     slots = lambda count: pltpu.VMEM((lanes, n - 1, count, chunk, lane_cols), bf16)
+    first_slot = lambda count: pltpu.VMEM((lanes, count, chunk, lane_cols), bf16)
     dma = pltpu.SemaphoreType.DMA
     vmem = pl.BlockSpec(memory_space=pltpu.VMEM)
     hbm = pl.BlockSpec(memory_space=pl.ANY)
@@ -372,12 +415,12 @@
             pltpu.VMEM((tokens, depth), bf16),
             pltpu.VMEM((depth, tokens), bf16),
             pltpu.VMEM((dp, rows, wide), bf16),
-            pltpu.VMEM((dp, rows, wide), jnp.float32),
+            pltpu.VMEM((dp, rows, wide), bf16),
             pltpu.VMEM((dp, dp, 2, rows // LEN, LEN), jnp.float32),
-            pltpu.VMEM((depth, wide), jnp.float32),
+            pltpu.VMEM((3, stage_rows(depth), wide), jnp.float32),
             pltpu.VMEM((depth, wide), bf16),
-            slots(2), slots(2), slots(dp - 2), slots(dp - 2),
-            dma((depth // stage_rows(depth),)),
+            slots(2), first_slot(2), slots(dp - 2), first_slot(dp - 2),
+            dma((3,)),
             dma,
             dma((dp - 1,)), dma((dp - 1,)),
             dma((2, lanes, 2 * n - 2)), dma((2, lanes, 2 * n - 2)),
@@ -385,7 +428,7 @@
             dma((dp + 1,)),
         ],
         compiler_params=pltpu.CompilerParams(
-            collective_id=0, has_side_effects=True, vmem_limit_bytes=60 * MIB
+            collective_id=0, has_side_effects=True, vmem_limit_bytes=34 * MIB
         ),
         cost_estimate=pl.CostEstimate(
             flops=2 * tokens * depth * wide, bytes_accessed=4 * depth * wide + 4 * tokens * depth,

time: 175 us -> 174 us (level)
  Pallas kernels: 168 us -> 154 us
  local copies, waits for them, and re-layouts: 3.28 us -> 16.7 us
    unnamed x7 -> x17, local copies, waits for them, and re-layouts: 2.83 us -> 16.2 us
    pallas_call x1, Pallas kernels: 45.9 us -> 37.6 us  [update(): pl.pallas_call(update_kernel, grid=(wide // cols, ff // tile), in_specs=[...]
    pallas_call x1, Pallas kernels: 122 us -> 117 us  [forward(): pl.pallas_call(functools.partial(forward_kernel, dp, n, lanes), in_specs=...]
where the time goes in v4:
time: 174 us; the launch traced here: 173 us
  Pallas kernels  154 us (89%)
  local copies, waits for them, and re-layouts  16.7 us (10%)
    pallas_call x1, Pallas kernels, forward(): pl.pallas_call(functools.partial(forward_kernel, dp, n, lanes), in_specs=...  117 us
    pallas_call x1, Pallas kernels, update(): pl.pallas_call(update_kernel, grid=(wide // cols, ff // tile), in_specs=[...  37.6 us
    unnamed x17, local copies, waits for them, and re-layouts  16.2 us

profile of v4, /device:TPU:0, one launch (start us, length us, event | category | flops | bytes accessed | tf_op | source)
XLA Modules:
  0.0 173.3 jit_solution(13823478709747811885)
XLA Ops:
  0.6 0.0 copy-start.7
  0.6 0.8 copy.23
  1.4 0.1 lt.29
  1.5 0.7 mul.16
  2.2 0.0 copy-start.5
  2.2 1.2 copy-done.5
  3.4 0.0 copy-start.6
  3.4 1.0 copy-done.6
  4.4 116.8 %shard_map.120 = (bf16[1792,1024]{1,0:T(8,128)(2,1)S(1)}, bf16[1024,2048]{1,0:T(8,128)(2,1)S(1)}, f32[4,2,2,128]{3,2,1,0:T(2,128)S(1)}) custom-call(bf16[256,1792]{1,0:T(8,128)(2,1)S(1)} %copy-done.5, bf16[128,2048]{1,0:T(8,128)(2,1)S(1)} %copy-done.6, f32[1,2048]{1,0:T(1,128)S(1)} %bitcast.6, f32[1792,2048]{1,0:T(8,128)} %p_ref.1), custom_call_target="tpu_custom_call" | custom-call | flops 7516192768 | bytes 22020096 | tf_op jit(solution)/shard_map/pallas_call | solution.py:405
  121.2 0.0 copy-start.1
  121.2 2.0 %copy-done.1 = bf16[1024,2048]{1,0:T(8,128)(2,1)} copy-done((bf16[1024,2048]{1,0:T(8,128)(2,1)}, bf16[1024,2048]{1,0:T(8,128)(2,1)S(1)}, u32[]{:S(2)}) %copy-start.1) | copy-done | bytes 4194328
  123.2 1.8 %copy-done.3 = bf16[1792,1024]{1,0:T(8,128)(2,1)} copy-done((bf16[1792,1024]{1,0:T(8,128)(2,1)}, bf16[1792,1024]{1,0:T(8,128)(2,1)S(1)}, u32[]{:S(2)}) %copy-start.3) | copy-done | bytes 3670040
  125.1 0.2 fusion.6
  125.2 0.2 slice_reduce_fusion
  125.4 0.0 copy-done.7
  125.4 0.6 fusion.4
  126.1 0.1 copy.26
  126.2 0.1 reshape.50
  126.3 0.1 select_multiply_fusion
  126.3 0.0 copy-start
  126.3 5.2 %copy-done = f32[1792,2048]{1,0:T(8,128)S(1)} copy-done((f32[1792,2048]{1,0:T(8,128)S(1)}, f32[1792,2048]{1,0:T(8,128)}, u32[]{:S(2)}) %copy-start) | copy-done | bytes 14680088
  131.5 2.2 %copy-done.2 = bf16[1024,2048]{1,0:T(8,128)(2,1)S(1)} copy-done((bf16[1024,2048]{1,0:T(8,128)(2,1)S(1)}, bf16[1024,2048]{1,0:T(8,128)(2,1)}, u32[]{:S(2)}) %copy-start.2) | copy-done | bytes 4194328
  133.7 2.0 %copy-done.4 = bf16[1792,1024]{1,0:T(8,128)(2,1)S(1)} copy-done((bf16[1792,1024]{1,0:T(8,128)(2,1)S(1)}, bf16[1792,1024]{1,0:T(8,128)(2,1)}, u32[]{:S(2)}) %copy-start.4) | copy-done | bytes 3670040
  135.7 37.6 %shard_map.121 = (f32[1792,2048]{1,0:T(8,128)}, f32[1792,2048]{1,0:T(8,128)}, f32[1792,2048]{1,0:T(8,128)}) custom-call(bf16[1792,1024]{1,0:T(8,128)(2,1)S(1)} %copy-done.4, bf16[1024,2048]{1,0:T(8,128)(2,1)S(1)} %copy-done.2, f32[8,128]{1,0:T(8,128)S(1)} %get-tuple-element.26.a_ref, f32[8,128]{1,0:T(8,128)S(1)} %get-tuple-element.25.b_ref, ...), custom_call_target="tpu_custom_call" | custom-call | flops 7516192768 | bytes 88080384 | tf_op jit(solution)/shard_map/pallas_call | solution.py:58
  (7 shorter events, 0.0 us)
Async XLA Ops:
  0.6 124.8 %copy-start.7 = (s32[4]{0:T(128)S(1)}, s32[4]{0:T(128)}, u32[]{:S(2)}) copy-start(s32[4]{0:T(128)} %param.17) | copy-start | bytes 52
  2.2 1.2 copy-start.5
  3.4 1.0 copy-start.6
  121.2 2.0 %copy-start.1 = (bf16[1024,2048]{1,0:T(8,128)(2,1)}, bf16[1024,2048]{1,0:T(8,128)(2,1)S(1)}, u32[]{:S(2)}) copy-start(bf16[1024,2048]{1,0:T(8,128)(2,1)S(1)} %get-tuple-element.11.s_ref) | copy-start | bytes 12582916
  123.2 1.8 %copy-start.3 = (bf16[1792,1024]{1,0:T(8,128)(2,1)}, bf16[1792,1024]{1,0:T(8,128)(2,1)S(1)}, u32[]{:S(2)}) copy-start(bf16[1792,1024]{1,0:T(8,128)(2,1)S(1)} %get-tuple-element.10.ht_ref) | copy-start | bytes 11010052
  126.3 5.2 %copy-start = (f32[1792,2048]{1,0:T(8,128)S(1)}, f32[1792,2048]{1,0:T(8,128)}, u32[]{:S(2)}) copy-start(f32[1792,2048]{1,0:T(8,128)} %p_ref.1) | copy-start | bytes 44040196
  131.5 2.2 %copy-start.2 = (bf16[1024,2048]{1,0:T(8,128)(2,1)S(1)}, bf16[1024,2048]{1,0:T(8,128)(2,1)}, u32[]{:S(2)}) copy-start(bf16[1024,2048]{1,0:T(8,128)(2,1)} %copy-done.1) | copy-start | bytes 12582916
  133.7 2.0 %copy-start.4 = (bf16[1792,1024]{1,0:T(8,128)(2,1)S(1)}, bf16[1792,1024]{1,0:T(8,128)(2,1)}, u32[]{:S(2)}) copy-start(bf16[1792,1024]{1,0:T(8,128)(2,1)} %copy-done.3) | copy-start | bytes 11010052

commit v5 on v4

--- a/solution.py
+++ b/solution.py
@@ -66,7 +66,7 @@
         out_specs=[state] * 3,
         out_shape=[out] * 3,
         scratch_shapes=[pltpu.VMEM((tokens, cols), jnp.bfloat16)],
-        compiler_params=pltpu.CompilerParams(vmem_limit_bytes=20 * MIB),
+        compiler_params=pltpu.CompilerParams(vmem_limit_bytes=48 * MIB),
         cost_estimate=pl.CostEstimate(
             flops=2 * tokens * ff * wide, bytes_accessed=24 * ff * wide, transcendentals=ff * wide
         ),

time: 174 us -> 174 us (level)
  Pallas kernels: 154 us -> 163 us
  local copies, waits for them, and re-layouts: 16.7 us -> 9.25 us
    pallas_call x1, Pallas kernels: 37.6 us -> 45.9 us  [update(): pl.pallas_call(update_kernel, grid=(wide // cols, ff // tile), in_specs=[...]
    unnamed x17 -> x13, local copies, waits for them, and re-layouts: 16.2 us -> 8.81 us
where the time goes in v5:
time: 174 us
  Pallas kernels  163 us (94%)
  local copies, waits for them, and re-layouts  9.25 us (5%)
    pallas_call x1, Pallas kernels, forward(): pl.pallas_call(functools.partial(forward_kernel, dp, n, lanes), in_specs=...  117 us
    pallas_call x1, Pallas kernels, update(): pl.pallas_call(update_kernel, grid=(wide // cols, ff // tile), in_specs=[...  45.9 us
    unnamed x13, local copies, waits for them, and re-layouts  8.81 us

profile of v5, /device:TPU:0, one launch (start us, length us, event | category | flops | bytes accessed | tf_op | source)
XLA Modules:
  0.0 174.2 jit_solution(15303191302572204837)
XLA Ops:
  0.6 0.0 copy-start.5
  0.6 0.8 copy.23
  1.4 0.1 lt.29
  1.5 0.7 mul.16
  2.2 0.0 copy-start.3
  2.2 1.2 copy-done.3
  3.4 0.0 copy-start.4
  3.4 1.0 copy-done.4
  4.4 116.8 %shard_map.120 = (bf16[1792,1024]{1,0:T(8,128)(2,1)S(1)}, bf16[1024,2048]{1,0:T(8,128)(2,1)S(1)}, f32[4,2,2,128]{3,2,1,0:T(2,128)S(1)}) custom-call(bf16[256,1792]{1,0:T(8,128)(2,1)S(1)} %copy-done.3, bf16[128,2048]{1,0:T(8,128)(2,1)S(1)} %copy-done.4, f32[1,2048]{1,0:T(1,128)S(1)} %bitcast.6, f32[1792,2048]{1,0:T(8,128)} %p_ref.1), custom_call_target="tpu_custom_call" | custom-call | flops 7516192768 | bytes 22020096 | tf_op jit(solution)/shard_map/pallas_call | solution.py:405
  121.2 0.0 copy-start
  121.2 1.9 %copy-done = bf16[1024,2048]{1,0:T(8,128)(2,1)} copy-done((bf16[1024,2048]{1,0:T(8,128)(2,1)}, bf16[1024,2048]{1,0:T(8,128)(2,1)S(1)}, u32[]{:S(2)}) %copy-start) | copy-done | bytes 4194328
  123.1 0.0 copy-start.1
  123.1 1.8 %copy-done.1 = bf16[1792,1024]{1,0:T(8,128)(2,1)} copy-done((bf16[1792,1024]{1,0:T(8,128)(2,1)}, bf16[1792,1024]{1,0:T(8,128)(2,1)S(1)}, u32[]{:S(2)}) %copy-start.1) | copy-done | bytes 3670040
  125.0 0.2 fusion.6
  125.1 0.2 slice_reduce_fusion
  125.3 0.0 copy-done.5
  125.3 0.6 fusion.4
  126.0 0.1 copy.26
  126.1 0.1 reshape.50
  126.2 0.1 select_multiply_fusion
  126.2 0.0 copy-start.2
  126.2 2.0 %copy-done.2 = bf16[1792,1024]{1,0:T(8,128)(2,1)S(1)} copy-done((bf16[1792,1024]{1,0:T(8,128)(2,1)S(1)}, bf16[1792,1024]{1,0:T(8,128)(2,1)}, u32[]{:S(2)}) %copy-start.2) | copy-done | bytes 3670040
  128.3 45.9 %shard_map.121 = (f32[1792,2048]{1,0:T(8,128)}, f32[1792,2048]{1,0:T(8,128)}, f32[1792,2048]{1,0:T(8,128)}) custom-call(bf16[1792,1024]{1,0:T(8,128)(2,1)S(1)} %copy-done.2, bf16[1024,2048]{1,0:T(8,128)(2,1)} %copy-done, f32[8,128]{1,0:T(8,128)S(1)} %get-tuple-element.26.a_ref, f32[8,128]{1,0:T(8,128)S(1)} %get-tuple-element.25.b_ref, ...), custom_call_target="tpu_custom_call" | custom-call | flops 7516192768 | bytes 88080384 | tf_op jit(solution)/shard_map/pallas_call | solution.py:58
  (4 shorter events, 0.0 us)
Async XLA Ops:
  0.6 124.7 %copy-start.5 = (s32[4]{0:T(128)S(1)}, s32[4]{0:T(128)}, u32[]{:S(2)}) copy-start(s32[4]{0:T(128)} %param.17) | copy-start | bytes 52
  2.2 1.2 copy-start.3
  3.4 1.0 copy-start.4
  121.2 1.9 %copy-start = (bf16[1024,2048]{1,0:T(8,128)(2,1)}, bf16[1024,2048]{1,0:T(8,128)(2,1)S(1)}, u32[]{:S(2)}) copy-start(bf16[1024,2048]{1,0:T(8,128)(2,1)S(1)} %get-tuple-element.11.s_ref) | copy-start | bytes 12582916
  123.1 1.8 %copy-start.1 = (bf16[1792,1024]{1,0:T(8,128)(2,1)}, bf16[1792,1024]{1,0:T(8,128)(2,1)S(1)}, u32[]{:S(2)}) copy-start(bf16[1792,1024]{1,0:T(8,128)(2,1)S(1)} %get-tuple-element.10.ht_ref) | copy-start | bytes 11010052
  126.2 2.0 %copy-start.2 = (bf16[1792,1024]{1,0:T(8,128)(2,1)S(1)}, bf16[1792,1024]{1,0:T(8,128)(2,1)}, u32[]{:S(2)}) copy-start(bf16[1792,1024]{1,0:T(8,128)(2,1)} %copy-done.1) | copy-start | bytes 11010052
